TPU v7x, 512 devices: a whole 4x4x16 slice. The times are simulated.
512 devices in a mesh: section: 16 (over x, y), ctx: 32 (over z, core).
Axes of the slice: x: 4, y: 4, z: 16, core: 2. Of those that a mesh axis runs over, the one named last changes fastest.
Arguments:
- activations: bfloat16 [16, 4096, 1024], P('section', 'ctx'), may hold values from -6 to 6
- norm_gain: float32 [16, 1024], P('section'), may hold values from 0.5 to 1.5
- in_weight: bfloat16 [16, 1024, 3072], P('section', 'ctx'), may hold values from -0.1875 to 0.1875
- short_weight: float32 [16, 3, 3072], P('section'), may hold values from -1 to 1
- long_filter: float32 [16, 1024, 4096], P('section', 'ctx'), may hold values from -1.2 to 1.2, as said below
- out_weight: bfloat16 [16, 1024, 1024], P('section', None, 'ctx'), may hold values from -0.1875 to 0.1875
Outputs:
- block_out: bfloat16 [16, 4096, 1024], P('section', 'ctx')
Inputs may be any that keep to these rules, and one draw needn't show every extreme that they name: `long_filter`: a causal filter whose magnitude falls with the lag at a rate that varies over channels.
All inputs are finite; a program needn't handle non-finite values.
Results may differ from a plain program's by a relative error of at most 0.0051.
Values may be sent and summed in bfloat16 or wider, within the bound.
A program may use at most 64 MiB of HBM per device.

v0:
```python
import math

import jax
import jax.numpy as jnp
from jax import lax
from jax.sharding import PartitionSpec as P

highest = lax.Precision.HIGHEST


def from_behind(value, axis, steps):
    count = lax.axis_size(axis)
    pairs = [(source, (source + steps) % count) for source in range(count)]
    return lax.ppermute(value, axis, pairs)


def shifted(value, axis, steps):
    count = lax.axis_size(axis)
    leading, last = (max(0, -steps), min(count, count - steps))
    return lax.ppermute(value, axis, [(source, source + steps) for source in range(leading, last)])


def rms_rows(rows, gain_row):
    values = rows.astype(jnp.float32)
    scale = lax.rsqrt(jnp.mean(values * values, axis=-1, keepdims=True) + 1e-06)
    return (values * scale * gain_row).astype(jnp.bfloat16)


def make_tables(parts, block):
    outer = 2 * parts
    total = outer * block
    k_index = jnp.arange(outer, dtype=jnp.int32)[:, None]
    n_index = jnp.arange(parts, dtype=jnp.int32)[None, :]
    b_index = jnp.arange(block, dtype=jnp.int32)
    outer_angle = 2.0 * math.pi / outer * (k_index * n_index % outer).astype(jnp.float32)
    twist_angle = 2.0 * math.pi / total * (k_index * b_index[None, :] % total).astype(jnp.float32)
    inner_angle = (
        2.0 * math.pi / block * (b_index[:, None] * b_index[None, :] % block).astype(jnp.float32)
    )
    return (
        jnp.cos(outer_angle),
        jnp.sin(outer_angle),
        jnp.cos(twist_angle),
        jnp.sin(twist_angle),
        jnp.cos(inner_angle),
        jnp.sin(inner_angle),
    )


def forward_dft(signal, tables, parts, block):
    cos_outer, sin_outer, cos_twist, sin_twist, cos_inner, sin_inner = tables
    shaped = signal.reshape(signal.shape[0], parts, block)
    real_a = jnp.einsum("kn,cnb->ckb", cos_outer, shaped, precision=highest)
    imag_a = -jnp.einsum("kn,cnb->ckb", sin_outer, shaped, precision=highest)
    real_b = real_a * cos_twist + imag_a * sin_twist
    imag_b = imag_a * cos_twist - real_a * sin_twist
    real_x = jnp.einsum("ckb,jb->ckj", real_b, cos_inner, precision=highest) + jnp.einsum(
        "ckb,jb->ckj", imag_b, sin_inner, precision=highest
    )
    imag_x = jnp.einsum("ckb,jb->ckj", imag_b, cos_inner, precision=highest) - jnp.einsum(
        "ckb,jb->ckj", real_b, sin_inner, precision=highest
    )
    return (real_x, imag_x)


def inverse_dft(real_y, imag_y, tables, parts, block):
    cos_outer, sin_outer, cos_twist, sin_twist, cos_inner, sin_inner = tables
    real_z = jnp.einsum("ckj,jb->ckb", real_y, cos_inner, precision=highest) - jnp.einsum(
        "ckj,jb->ckb", imag_y, sin_inner, precision=highest
    )
    imag_z = jnp.einsum("ckj,jb->ckb", imag_y, cos_inner, precision=highest) + jnp.einsum(
        "ckj,jb->ckb", real_y, sin_inner, precision=highest
    )
    real_w = real_z * cos_twist - imag_z * sin_twist
    imag_w = imag_z * cos_twist + real_z * sin_twist
    result = jnp.einsum("kn,ckb->cnb", cos_outer, real_w, precision=highest) - jnp.einsum(
        "kn,ckb->cnb", sin_outer, imag_w, precision=highest
    )
    return (result / (2.0 * parts * block)).reshape(real_y.shape[0], parts * block)


def long_convolution(channels, filter_rows, parts, block):
    tables = make_tables(parts, block)
    real_data, imag_data = forward_dft(channels.astype(jnp.float32), tables, parts, block)
    real_filt, imag_filt = forward_dft(filter_rows, tables, parts, block)
    real_prod = real_data * real_filt - imag_data * imag_filt
    imag_prod = real_data * imag_filt + imag_data * real_filt
    return inverse_dft(real_prod, imag_prod, tables, parts, block)


def shards(activations, norm_gain, in_weight, short_weight, long_filter, out_weight):
    inputs = from_behind(activations, "section", 1)[0]
    gain_row = norm_gain[0]
    tok_rows = inputs.shape[0]
    model_width = inputs.shape[1]
    parts = lax.axis_size("ctx")
    normed = rms_rows(inputs, gain_row)
    own_features = lax.dot_general(
        lax.all_gather(in_weight, "ctx", axis=1, tiled=True)[0],
        normed,
        (((0,), (1,)), ((), ())),
        preferred_element_type=jnp.float32,
    )
    prior_features = shifted(own_features[:, tok_rows - 2 :], "ctx", 1)
    features = jnp.concatenate([prior_features, own_features], axis=1)
    taps = short_weight[0]
    mixed = (
        taps[0][:, None] * features[:, 2:]
        + taps[1][:, None] * features[:, 1:-1]
        + taps[2][:, None] * features[:, :-2]
    )
    query_side = mixed[:model_width]
    key_side = mixed[model_width : 2 * model_width]
    value_side = mixed[2 * model_width :]
    product = (key_side * value_side).astype(jnp.bfloat16)
    channels = lax.all_to_all(product, "ctx", split_axis=0, concat_axis=1, tiled=True)
    conv = long_convolution(channels, long_filter[0], parts, tok_rows).astype(jnp.bfloat16)
    returned = lax.all_to_all(conv, "ctx", split_axis=1, concat_axis=0, tiled=True)
    gated = (query_side * returned.astype(jnp.float32)).astype(jnp.bfloat16)
    mixing = lax.dot_general(
        gated,
        lax.all_gather(out_weight, "ctx", axis=2, tiled=True)[0],
        (((0,), (0,)), ((), ())),
        preferred_element_type=jnp.float32,
    )
    return (inputs.astype(jnp.float32) + mixing).astype(jnp.bfloat16)[None]


def solution(mesh):
    return jax.shard_map(
        shards,
        mesh=mesh,
        in_specs=(
            P("section", "ctx", None),
            P("section", None),
            P("section", "ctx", None),
            P("section", None, None),
            P("section", "ctx", None),
            P("section", None, "ctx"),
        ),
        out_specs=P("section", "ctx", None),
        check_vma=False,
    )
```

profile of v0, /device:TPU:1, one launch (start us, length us, event | category | flops | bytes accessed | tf_op | source)
XLA Modules:
  0.0 188.5 jit_solution(15882375859539556635)
XLA Ops:
  7.3 4.0 %collective-permute-start = (bf16[1,128,1024]{2,1,0:T(8,128)(2,1)}, bf16[1,128,1024]{2,1,0:T(8,128)(2,1)S(1)}, u32[]{:S(2)}, u32[]{:S(2)}) collective-permute-start(bf16[1,128,1024]{2,1,0:T(8,128)(2,1)} %param.6), channel_id=1, source_target_pairs={{0,32},{32,64},{64,96},{96,128},{128,160},{160,192},{192,224},{224... | collective-permute-start | bytes 786440 | tf_op jit(solution)/shard_map/ppermute | solution.py:14
  15.5 3.5 %collective-permute-done = bf16[1,128,1024]{2,1,0:T(8,128)(2,1)S(1)} collective-permute-done((bf16[1,128,1024]{2,1,0:T(8,128)(2,1)}, bf16[1,128,1024]{2,1,0:T(8,128)(2,1)S(1)}, u32[]{:S(2)}, u32[]{:S(2)}) %collective-permute-start) | collective-permute-done | bytes 262176 | tf_op jit(solution)/shard_map/ppermute | solution.py:14
  19.1 73.1 %all-gather.3.cloned.1.call-done = bf16[1,1024,3072]{2,1,0:T(8,128)(2,1)} async-done(((bf16[1,32,3072]{2,1,0:T(8,128)(2,1)}), bf16[1,1024,3072]{2,1,0:T(8,128)(2,1)}) %all-gather.3.cloned.1.call-update) | async-done | bytes 6291472 | tf_op jit(solution)/shard_map/all_gather | solution.py:99
  92.1 3.8 %fusion.2 = f32[3072,128]{0,1:T(8,128)S(1)} fusion(bf16[1,1024,3072]{2,1,0:T(8,128)(2,1)} %all-gather.3.cloned.1.call-done, bf16[1,128,1024]{2,1,0:T(8,128)(2,1)S(1)} %collective-permute-done, f32[1024]{0:T(1024)S(1)} %bitcast.113, f32[128]{0:T(128)S(1)} %add_rsqrt_fusion), kind=kOutput, calls=%fused_computation.2 | convolution fusion | flops 805830656 | bytes 8131072 | tf_op jit(solution)/shard_map/dot_general | solution.py:98
  96.0 3.6 %collective-permute-start.1 = (f32[3072,2]{0,1:T(2,128)S(1)}, f32[3072,2]{0,1:T(2,128)S(1)}, u32[]{:S(2)}, u32[]{:S(2)}) collective-permute-start(f32[3072,2]{0,1:T(2,128)S(1)} %slice.39), channel_id=1, source_target_pairs={{0,1},{1,2},{2,3},{3,4},{4,5},{5,6},{6,7},{7,8},{8,9},{9,10},{10,1... | collective-permute-start | bytes 73736 | tf_op jit(solution)/shard_map/ppermute | solution.py:20
  101.0 1.2 copy-done
  103.1 10.4 %all-to-all-start = ((bf16[32,32,128]{2,1,0:T(8,128)(2,1)}), bf16[32,32,128]{2,1,0:T(8,128)(2,1)}, u32[]{:S(2)}, u32[]{:S(2)}) async-start(bf16[32,32,128]{2,1,0:T(8,128)(2,1)} %bitcast.8), calls=%async_computation | async-start | bytes 524288 | tf_op jit(solution)/shard_map/all_to_all | solution.py:116
  113.5 1.2 fusion.29
  114.8 1.2 fusion.25
  116.0 1.2 convolution_add_fusion.1
  117.3 2.2 %convolution_subtract_fusion.1 = f32[32,64,128]{2,1,0:T(8,128)} fusion(f32[32,64,128]{2,1,0:T(8,128)S(1)} %fusion.25, f32[64,32,128]{2,0,1:T(8,128)S(1)} %convolution_negate_fusion, f32[64,32,128]{2,0,1:T(8,128)S(1)} %fusion.106, f32[64,128]{1,0:T(8,128)S(1)} %get-tuple-element.10, f32[64,128]{1,0:T(8,128)S(1)} %get-tuple-element.11), kind=kOutput, calls=%fused_computation.16 | convolution fusion | flops 403931136 | bytes 4259840 | tf_op jit(solution)/shard_map/ckb,jb->ckj/dot_general | solution.py:60
  119.5 18.3 %all-to-all-done = bf16[32,32,128]{2,1,0:T(8,128)(2,1)} async-done(((bf16[32,32,128]{2,1,0:T(8,128)(2,1)}), bf16[32,32,128]{2,1,0:T(8,128)(2,1)}, u32[]{:S(2)}, u32[]{:S(2)}) %all-to-all-start) | async-done | bytes 262176 | tf_op jit(solution)/shard_map/all_to_all | solution.py:116
  137.8 1.7 convolution_bitcast_fusion
  139.4 1.6 fusion.12
  141.1 1.2 fusion.48
  142.3 1.3 fusion.49
  143.6 1.3 convolution_add_fusion.2
  144.9 1.5 multiply_subtract_fusion
  146.4 1.5 fusion.70
  147.9 1.2 fusion.68
  149.1 1.2 convolution_subtract_fusion
  150.3 1.2 convolution_add_fusion
  153.5 24.5 %all_to_all.26 = bf16[32,32,128]{2,0,1:T(8,128)(2,1)S(1)} all-to-all(bf16[32,32,128]{2,0,1:T(8,128)(2,1)S(1)} %copy.15), channel_id=1, replica_groups=mesh['section'=16,'ctx'=32] {'ctx'}, dimensions={1} | all-to-all | bytes 524288 | tf_op jit(solution)/shard_map/all_to_all | solution.py:118
  178.3 3.3 %fusion.21 = bf16[1,128,1024]{2,1,0:T(8,128)(2,1)} fusion(bf16[1,1024,1024]{1,2,0:T(8,128)(2,1)} %all-gather.5.cloned.1.call-done, bf16[1,128,1024]{2,1,0:T(8,128)(2,1)S(1)} %collective-permute-done, f32[1024,128]{0,1:T(8,128)S(1)} %copy.16, f32[3072,128]{0,1:T(8,128)} %copy-done), kind=kOutput, calls=%fused_computation.28 | convolution fusion | flops 269090816 | bytes 3670016 | tf_op jit(solution)/shard_map/dot_general | solution.py:120
  (27 shorter events, 9.5 us)
Async XLA Ops:
  6.5 85.6 %all-gather.3.cloned.1.call-start = ((), (), s32[]{:S(2)}) async-start(), calls=%async_computation.2 | async-start | bytes 6488064 | tf_op jit(solution)/shard_map/all_gather | solution.py:99
  7.3 171.0 %all-gather.5.cloned.1.call-start = ((), (), s32[]{:S(2)}) async-start(), calls=%async_computation.3 | async-start | bytes 2162688 | tf_op jit(solution)/shard_map/all_gather | solution.py:122
  7.3 11.6 %collective-permute-start = (bf16[1,128,1024]{2,1,0:T(8,128)(2,1)}, bf16[1,128,1024]{2,1,0:T(8,128)(2,1)S(1)}, u32[]{:S(2)}, u32[]{:S(2)}) collective-permute-start(bf16[1,128,1024]{2,1,0:T(8,128)(2,1)} %param.6), channel_id=1, source_target_pairs={{0,32},{32,64},{64,96},{96,128},{128,160},{160,192},{192,224},{224... | collective-permute-start | bytes 786440 | tf_op jit(solution)/shard_map/ppermute | solution.py:14
  13.3 78.9 %copy-start.2 = (f32[1,1024]{1,0:T(1,128)S(1)}, f32[1,1024]{1,0:T(1,128)}, u32[]{:S(2)}) copy-start(f32[1,1024]{1,0:T(1,128)} %param.7) | copy-start | bytes 12292
  96.0 4.6 %collective-permute-start.1 = (f32[3072,2]{0,1:T(2,128)S(1)}, f32[3072,2]{0,1:T(2,128)S(1)}, u32[]{:S(2)}, u32[]{:S(2)}) collective-permute-start(f32[3072,2]{0,1:T(2,128)S(1)} %slice.39), channel_id=1, source_target_pairs={{0,1},{1,2},{2,3},{3,4},{4,5},{5,6},{6,7},{7,8},{8,9},{9,10},{10,1... | collective-permute-start | bytes 73736 | tf_op jit(solution)/shard_map/ppermute | solution.py:20
  101.0 1.2 copy-start
  103.1 34.7 %all-to-all-start = ((bf16[32,32,128]{2,1,0:T(8,128)(2,1)}), bf16[32,32,128]{2,1,0:T(8,128)(2,1)}, u32[]{:S(2)}, u32[]{:S(2)}) async-start(bf16[32,32,128]{2,1,0:T(8,128)(2,1)} %bitcast.8), calls=%async_computation | async-start | bytes 524288 | tf_op jit(solution)/shard_map/all_to_all | solution.py:116
  143.6 1.3 copy-start.1
Sparse Core Ops, SparseCore 0:
  9.5 82.6 all-gather.2
  94.2 76.0 all-gather.4
where the time goes:
time: 189 us; the launch traced here: 188 us
  waiting for transfers between devices  96.3 us (51%)
  matrix products  30.7 us (16%)
  blocking collectives  24.5 us (13%)
  starting transfers between devices  18.1 us (10%)
  between operations  13.6 us (7%)
  local copies, waits for them, and re-layouts  4.2 us (2%)
    all_gather x1, waiting for transfers between devices, shards(): lax.all_gather(in_weight, 'ctx', axis=1, tiled=True)[0]  73.1 us
    all_to_all x1, blocking collectives, shards(): lax.all_to_all(conv, 'ctx', split_axis=1, concat_axis=0, tiled=True)  24.5 us
    all_to_all x1, waiting for transfers between devices, shards(): lax.all_to_all(product, 'ctx', split_axis=0, concat_axis=1, tiled=True)  18.3 us
    all_to_all x1, starting transfers between devices, shards(): lax.all_to_all(product, 'ctx', split_axis=0, concat_axis=1, tiled=True)  10.4 us
    ppermute x1, starting transfers between devices, from_behind(): return lax.ppermute(value, axis, pairs)  4.03 us
    dot_general x1, matrix products, shards(): lax.dot_general(lax.all_gather(in_weight, 'ctx', axis=1, tiled=True)[0],...  3.83 us
  transfers between devices with their start and end apart: 5, of which 4 were waited for; matrix products, arithmetic and copies ran while one was open for 17% of the time, Pallas kernels for 0%

commit v1 on v0

v1 whole, which is shorter than its diff:
```python
import functools
import math

import jax
import jax.numpy as jnp
import numpy as np
from jax import lax
from jax.experimental import pallas as pl
from jax.experimental.pallas import tpu as pltpu
from jax.sharding import PartitionSpec as P

MESH = pl.DeviceIdType.MESH
F32, BF16 = jnp.float32, jnp.bfloat16
HALO = 16
HALF = 16


def transform_tables(parts, block):
    points = parts * block
    k = np.arange(parts)[:, None] + 0.25
    outer = 2.0 * math.pi * k * np.arange(parts)[None, :] / parts
    eye = np.eye(HALF)
    forward = np.concatenate([np.kron(np.cos(outer), eye), np.kron(-np.sin(outer), eye)], axis=0)
    inner = 2.0 * math.pi * np.outer(np.arange(block), np.arange(block)) / block
    cos, sin = np.cos(inner), np.sin(inner)
    inner_forward = np.block([[cos, -sin], [sin, cos]])
    inner_inverse = np.block([[cos, sin], [-sin, cos]])
    twist = np.repeat(2.0 * math.pi * k * np.arange(block)[None, :] / points, HALF, axis=0)
    tables = (forward, forward.T, inner_forward, inner_inverse, np.cos(twist), np.sin(twist))
    return [np.asarray(table, np.float32) for table in tables]


def split(value):
    high = value.astype(BF16)
    return high, (value - high.astype(F32)).astype(BF16)


def dot(a, b):
    return jnp.dot(a, b, preferred_element_type=F32)


def dot3(a_high, a_low, b_high, b_low):
    return dot(a_high, b_high) + (dot(a_high, b_low) + dot(a_low, b_high))


def kernel(
    sections, chips, width, tokens,
    act, gain, in_w, taps, filt, out_w, g_in, gi_in, d_in, di_in, tw_cos_in, tw_sin_in,
    out,
    w, rows_in, halo_in, normed, feat, prod, chan, query, outer, spec, back_hi, back_lo, conv, ret,
    fil, g_all, gi_all, d_all, di_all, tw_cos, tw_sin, g_hi, g_lo, gi_hi, gi_lo, d_hi, d_lo, di_hi, di_lo,
    ring_send, ring_recv, own_sem, relay_send, relay_recv, to_send, to_recv, back_send, back_recv,
    load_sem,
):
    parts = 2 * chips
    depth = width // parts
    block = tokens
    half_rows = parts * HALF
    tile = min(256, width)
    sec, me = lax.axis_index("section"), lax.axis_index("ctx")
    core = lax.rem(me, 2)
    chip = lax.div(me, 2)

    def at(chip_index, core_index):
        return lax.rem(chip_index + 2 * chips, chips) * 2 + core_index

    right, left, sibling = at(chip + 1, core), at(chip - 1, core), at(chip, 1 - core)
    next_sec, prev_sec = lax.rem(sec + 1, sections), lax.rem(sec + sections - 1, sections)
    next_ctx, prev_ctx = lax.rem(me + 1, parts), lax.rem(me + parts - 1, parts)

    loads = [
        pltpu.make_async_copy(source, target, load_sem.at[slot])
        for slot, (source, target) in enumerate(
            [
                (filt.at[0], fil), (g_in, g_all), (d_in, d_all), (tw_cos_in, tw_cos), (tw_sin_in, tw_sin),
                (di_in, di_all), (gi_in, gi_all),
            ]
        )
    ]
    for load in loads:
        load.start()

    barrier = pltpu.get_barrier_semaphore()

    def greet(offset, carry):
        peer = lax.rem(me + offset, parts)
        pl.semaphore_signal(barrier, inc=1, device_id=(sec, peer), device_id_type=MESH)
        return carry

    lax.fori_loop(1, parts, greet, 0)
    pl.semaphore_signal(barrier, inc=1, device_id=(prev_sec, me), device_id_type=MESH)
    pl.semaphore_signal(barrier, inc=1, device_id=(prev_sec, prev_ctx), device_id_type=MESH)
    pl.semaphore_wait(barrier, parts + 1)

    relay = pltpu.make_async_remote_copy(
        act.at[0], rows_in, relay_send.at[0], relay_recv.at[0],
        device_id=(next_sec, me), device_id_type=MESH,
    )
    relay_halo = pltpu.make_async_remote_copy(
        act.at[0, pl.ds(tokens - HALO, HALO)], halo_in, relay_send.at[1], relay_recv.at[1],
        device_id=(next_sec, next_ctx), device_id_type=MESH,
    )

    hops_right = chips // 2
    hops_left = chips - 1 - hops_right
    sources = [
        in_w.at[0, :, pl.ds(width, width)], in_w.at[0, :, pl.ds(2 * width, width)],
        in_w.at[0, :, pl.ds(0, width)], out_w.at[0],
    ]

    def slot(kind, owner):
        return w.at[kind, pl.ds(pl.multiple_of(owner * depth, depth), depth)]

    def ring_copy(kind, source, owner, target):
        return pltpu.make_async_remote_copy(
            source, slot(kind, owner), ring_send.at[kind], ring_recv.at[kind, owner],
            device_id=(sec, target), device_id_type=MESH,
        )

    def arrived(kind, owner):
        pltpu.make_async_copy(slot(kind, owner), slot(kind, owner), ring_recv.at[kind, owner]).wait()

    def ring_start(kind):
        if hops_right:
            ring_copy(kind, sources[kind], me, right).start()
        if hops_left:
            ring_copy(kind, sources[kind], me, left).start()
        ring_copy(kind, sources[kind], me, sibling).start()
        pltpu.make_async_copy(sources[kind], slot(kind, me), own_sem.at[kind]).start()

    def ring_step(kind, step):
        if step <= hops_right:
            owner = at(chip - step, core)
            arrived(kind, owner)
            if step < hops_right:
                ring_copy(kind, slot(kind, owner), owner, right).start()
            ring_copy(kind, slot(kind, owner), owner, sibling).start()
        if step <= hops_left:
            owner = at(chip + step, core)
            arrived(kind, owner)
            if step < hops_left:
                ring_copy(kind, slot(kind, owner), owner, left).start()
            ring_copy(kind, slot(kind, owner), owner, sibling).start()

    def ring_finish(kind):
        pltpu.make_async_copy(sources[kind], slot(kind, me), own_sem.at[kind]).wait()

        def other(index, carry):
            arrived(kind, 2 * index + 1 - core)
            return carry

        lax.fori_loop(0, chips, other, 0)

    ring_start(0)
    relay.start()
    relay_halo.start()
    ring_start(1)

    def outer_rows(index, columns_high, columns_low):
        rows = pl.ds(pl.multiple_of(index * tile_o, tile_o), tile_o)
        value = dot(g_hi[rows, :], columns_high) + dot(g_lo[rows, :], columns_high)
        if columns_low is not None:
            value = value + dot(g_hi[rows, :], columns_low)
        outer[rows, :] = value

    tile_o = min(256, 2 * half_rows)
    tile_i = min(256, half_rows)

    def inner_rows(group, index):
        rows = pl.ds(index * tile_i, tile_i)
        lanes = pl.ds(group * block, block)
        real = outer[rows, lanes]
        imag = outer[pl.ds(half_rows + index * tile_i, tile_i), lanes]
        cos, sin = tw_cos[rows, :], tw_sin[rows, :]
        turned = jnp.concatenate([real * cos + imag * sin, imag * cos - real * sin], axis=1)
        high, low = split(turned)
        return dot3(high, low, d_hi[...], d_lo[...])

    groups = depth // HALF
    inner_tiles = half_rows // tile_i
    outer_tiles = 2 * half_rows // tile_o

    def filter_outer(first, count):
        pieces = []
        for group in range(groups):
            pieces.append(jnp.concatenate(
                [fil[pl.ds(group * HALF, HALF), pl.ds(n * block, block)] for n in range(parts)], axis=0
            ))
        high, low = split(jnp.concatenate(pieces, axis=1))
        for index in range(first, first + count):
            outer_rows(index, high, low)

    def filter_inner(group):
        for index in range(inner_tiles):
            spec[group, pl.ds(index * tile_i, tile_i), :] = inner_rows(group, index) * (1.0 / (parts * block))

    def norm(values, gain_row):
        values = values.astype(F32)
        scale = lax.rsqrt(jnp.mean(values * values, axis=-1, keepdims=True) + 1e-06)
        return values * scale * gain_row

    def norm_rows():
        relay.wait_recv()
        relay_halo.wait_recv()
        before = norm(halo_in[...], gain[...])
        normed[pl.ds(0, HALO), :] = jnp.where(me > 0, before, jnp.zeros_like(before)).astype(BF16)
        normed[pl.ds(HALO, tokens), :] = norm(rows_in[...], gain[...]).astype(BF16)

    def wait_loads(first, count):
        for load in loads[first : first + count]:
            load.wait()

    steps = max(hops_right, hops_left)
    def split_table(whole, high, low):
        high[...], low[...] = split(whole[...])

    between = [
        lambda: (wait_loads(0, 2), split_table(g_all, g_hi, g_lo)),
        lambda: filter_outer(0, outer_tiles // 2),
        lambda: filter_outer(outer_tiles // 2, outer_tiles - outer_tiles // 2),
        lambda: (wait_loads(2, 3), split_table(d_all, d_hi, d_lo), filter_inner(0)),
        lambda: [filter_inner(group) for group in range(1, groups)],
        norm_rows,
        lambda: (wait_loads(5, 2), split_table(di_all, di_hi, di_lo), split_table(gi_all, gi_hi, gi_lo)),
    ]
    for step in range(1, steps + 1):
        ring_step(0, step)
        ring_step(1, step)
        if between:
            between.pop(0)()
    for piece in between:
        piece()
    ring_start(2)
    ring_finish(0)
    ring_finish(1)

    def mixed(kind, column, place):
        columns = pl.ds(pl.multiple_of(column, tile), tile)
        feat[place] = dot(normed[...], w[kind, :, columns])
        base = (0 if kind == 2 else width * (kind + 1)) + column
        weights = [taps[i, :, pl.ds(pl.multiple_of(base, tile), tile)] for i in range(3)]
        value = weights[0] * feat[place, pl.ds(HALO, tokens), :]
        value = value + weights[1] * feat[place, pl.ds(HALO - 1, tokens), :]
        return value + weights[2] * feat[place, pl.ds(HALO - 2, tokens), :]

    tiles = width // tile
    per_tile = tile // depth

    def product_tile(index, carry):
        at_tile = lax.rem(lax.div(me, per_tile) + 1 + index, tiles)
        column = at_tile * tile
        value = (mixed(0, column, 0) * mixed(1, column, 1)).T.astype(BF16)
        first = pl.multiple_of(at_tile * per_tile, per_tile)
        prod[pl.ds(first, per_tile)] = value.reshape(per_tile, depth, tokens)

        def send(offset, inner):
            peer = first + offset

            @pl.when(peer != me)
            def _():
                pltpu.make_async_remote_copy(
                    prod.at[peer], chan.at[me], to_send, to_recv.at[me],
                    device_id=(sec, peer), device_id_type=MESH,
                ).start()

            return inner

        return lax.fori_loop(0, per_tile, send, carry)

    lax.fori_loop(0, tiles, product_tile, 0)
    chan[me] = prod[me]

    for step in range(1, steps + 1):
        ring_step(2, step)
    ring_start(3)
    ring_finish(2)

    def query_tile(index, carry):
        column = index * tile
        query[pl.ds(pl.multiple_of(column, tile), tile), :] = mixed(2, column, 0).T
        return carry

    lax.fori_loop(0, tiles, query_tile, 0)

    def to_here(offset, carry):
        peer = lax.rem(me + offset, parts)
        pltpu.make_async_copy(chan.at[peer], chan.at[peer], to_recv.at[peer]).wait()
        return carry

    lax.fori_loop(1, parts, to_here, 0)

    columns = jnp.concatenate(
        [chan[:, pl.ds(group * HALF, HALF), :].reshape(half_rows, block) for group in range(groups)], axis=1
    )
    for index in range(outer_tiles):
        outer_rows(index, columns, None)
    for group in range(groups):
        lanes = pl.ds(group * block, block)
        for index in range(inner_tiles):
            rows = pl.ds(index * tile_i, tile_i)
            data = inner_rows(group, index)
            real, imag = data[:, :block], data[:, block:]
            filter_real, filter_imag = spec[group, rows, pl.ds(0, block)], spec[group, rows, pl.ds(block, block)]
            product = jnp.concatenate(
                [real * filter_real - imag * filter_imag, real * filter_imag + imag * filter_real], axis=1
            )
            high, low = split(product)
            value = dot3(high, low, di_hi[...], di_lo[...])
            real, imag = value[:, :block], value[:, block:]
            cos, sin = tw_cos[rows, :], tw_sin[rows, :]
            high, low = split(real * cos - imag * sin)
            back_hi[rows, lanes], back_lo[rows, lanes] = high, low
            high, low = split(imag * cos + real * sin)
            below = pl.ds(half_rows + index * tile_i, tile_i)
            back_hi[below, lanes], back_lo[below, lanes] = high, low

    per_rows = tile_i // HALF
    back_tiles = half_rows // tile_i

    def conv_tile(index, carry):
        at_tile = lax.rem(lax.div(me, per_rows) + 1 + index, back_tiles)
        rows = pl.ds(pl.multiple_of(at_tile * tile_i, tile_i), tile_i)
        value = dot3(gi_hi[rows, :], gi_lo[rows, :], back_hi[...], back_lo[...]).astype(BF16)
        first = pl.multiple_of(at_tile * per_rows, per_rows)
        for group in range(groups):
            conv[pl.ds(first, per_rows), pl.ds(group * HALF, HALF), :] = value[
                :, group * block : (group + 1) * block
            ].reshape(per_rows, HALF, block)

        def send(offset, inner):
            peer = first + offset

            @pl.when(peer != me)
            def _():
                pltpu.make_async_remote_copy(
                    conv.at[peer], ret.at[me], back_send, back_recv.at[me],
                    device_id=(sec, peer), device_id_type=MESH,
                ).start()

            return inner

        return lax.fori_loop(0, per_rows, send, carry)

    lax.fori_loop(0, back_tiles, conv_tile, 0)
    ret[me] = conv[me]

    for step in range(1, steps + 1):
        ring_step(3, step)
    ring_finish(3)

    def back_here(offset, carry):
        peer = lax.rem(me + offset, parts)
        pltpu.make_async_copy(ret.at[peer], ret.at[peer], back_recv.at[peer]).wait()
        return carry

    lax.fori_loop(1, parts, back_here, 0)

    gated = (query[...] * ret[...].reshape(width, tokens).astype(F32)).astype(BF16)
    for index in range(tiles):
        span = pl.ds(index * tile, tile)
        mixing = dot(w[3, span, :], gated)
        out[0, :, span] = (rows_in[:, span].astype(F32) + mixing.T).astype(BF16)

    relay.wait_send()
    relay_halo.wait_send()
    sent = (hops_right + hops_left + chips) * depth
    for kind in range(4):
        all_sent = w.at[kind, pl.ds(0, sent)]
        pltpu.make_async_copy(all_sent, all_sent, ring_send.at[kind]).wait()
    others = prod.at[pl.ds(0, parts - 1)]
    pltpu.make_async_copy(others, others, to_send).wait()
    others = conv.at[pl.ds(0, parts - 1)]
    pltpu.make_async_copy(others, others, back_send).wait()


def shards(activations, norm_gain, in_weight, short_weight, long_filter, out_weight):
    sections, parts = lax.axis_size("section"), lax.axis_size("ctx")
    chips = parts // 2
    tokens, width = activations.shape[1:]
    depth = width // parts
    half_rows = parts * HALF
    lanes = depth // HALF * tokens
    tables = [jnp.asarray(table) for table in transform_tables(parts, tokens)]
    in_hbm = pl.BlockSpec(memory_space=pltpu.HBM)
    in_vmem = pl.BlockSpec(memory_space=pltpu.VMEM)
    tile = min(256, width)
    scratch = [
        pltpu.VMEM((4, width, width), BF16),
        pltpu.VMEM((tokens, width), BF16),
        pltpu.VMEM((HALO, width), BF16),
        pltpu.VMEM((HALO + tokens, width), BF16),
        pltpu.VMEM((2, HALO + tokens, tile), F32),
        pltpu.VMEM((parts, depth, tokens), BF16),
        pltpu.VMEM((parts, depth, tokens), BF16),
        pltpu.VMEM((width, tokens), F32),
        pltpu.VMEM((2 * half_rows, lanes), F32),
        pltpu.VMEM((depth // HALF, half_rows, 2 * tokens), F32),
        pltpu.VMEM((2 * half_rows, lanes), BF16),
        pltpu.VMEM((2 * half_rows, lanes), BF16),
        pltpu.VMEM((parts, depth, tokens), BF16),
        pltpu.VMEM((parts, depth, tokens), BF16),
        pltpu.VMEM(long_filter.shape[1:], F32),
        *[pltpu.VMEM(table.shape, F32) for table in tables],
        *[pltpu.VMEM(table.shape, BF16) for table in tables[:4] for _ in range(2)],
        pltpu.SemaphoreType.DMA((4,)),
        pltpu.SemaphoreType.DMA((4, parts)),
        pltpu.SemaphoreType.DMA((4,)),
        pltpu.SemaphoreType.DMA((2,)),
        pltpu.SemaphoreType.DMA((2,)),
        pltpu.SemaphoreType.DMA,
        pltpu.SemaphoreType.DMA((parts,)),
        pltpu.SemaphoreType.DMA,
        pltpu.SemaphoreType.DMA((parts,)),
        pltpu.SemaphoreType.DMA((len(tables) + 1,)),
    ]
    return pl.pallas_call(
        functools.partial(kernel, sections, chips, width, tokens),
        out_shape=jax.ShapeDtypeStruct(activations.shape, BF16),
        in_specs=[in_hbm, in_vmem, in_hbm, in_vmem] + [in_hbm] * (2 + len(tables)),
        out_specs=in_vmem,
        scratch_shapes=scratch,
        compiler_params=pltpu.CompilerParams(
            collective_id=0, has_side_effects=True, vmem_limit_bytes=63 * 1024 * 1024
        ),
    )(
        activations, norm_gain, in_weight, jnp.transpose(short_weight, (1, 0, 2)), long_filter,
        jnp.swapaxes(out_weight, 1, 2), *tables,
    )


def solution(mesh):
    return jax.shard_map(
        shards,
        mesh=mesh,
        in_specs=(
            P("section", "ctx", None),
            P("section", None),
            P("section", "ctx", None),
            P("section", None, None),
            P("section", "ctx", None),
            P("section", None, "ctx"),
        ),
        out_specs=P("section", "ctx", None),
        check_vma=False,
    )
```

time: 189 us -> 132 us (0.70)
  Pallas kernels: 0 us -> 130 us
  waiting for transfers between devices: 96.3 us -> 0 us
  matrix products: 30.7 us -> 0 us
  blocking collectives: 24.5 us -> 0 us
  starting transfers between devices: 18.1 us -> 0 us
  between operations: 13.6 us -> 0.01 us
  local copies, waits for them, and re-layouts: 4.2 us -> 1.67 us
    pallas_call x0 -> x1, Pallas kernels: none -> 130 us  [shards(): pl.pallas_call(functools.partial(kernel, sections, chips, width, tokens),...]
    all_gather x2 -> x0, waiting for transfers between devices: 73.1 us -> none  [the longest x1 73.1 us: shards(): lax.all_gather(in_weight, 'ctx', axis=1, tiled=True)[0]]
    dot_general x20 -> x0, matrix products: 30.7 us -> none  [the longest x1 3.83 us: shards(): lax.dot_general(lax.all_gather(in_weight, 'ctx', axis=1, tiled=True)[0],...]
    all_to_all x1 -> x0, blocking collectives: 24.5 us -> none  [shards(): lax.all_to_all(conv, 'ctx', split_axis=1, concat_axis=0, tiled=True)]
    all_to_all x1 -> x0, waiting for transfers between devices: 18.3 us -> none  [shards(): lax.all_to_all(product, 'ctx', split_axis=0, concat_axis=1, tiled=True)]
    all_to_all x1 -> x0, starting transfers between devices: 10.4 us -> none  [shards(): lax.all_to_all(product, 'ctx', split_axis=0, concat_axis=1, tiled=True)]
    ppermute x2 -> x0, starting transfers between devices: 7.66 us -> none  [the longest x1 4.03 us: from_behind(): return lax.ppermute(value, axis, pairs)]
    ppermute x2 -> x0, waiting for transfers between devices: 4.23 us -> none  [the longest x1 3.45 us: from_behind(): return lax.ppermute(value, axis, pairs)]
  transfers between devices with their start and end apart: 5 -> 0, of which waited for: 4 -> 0; matrix products, arithmetic and copies ran while one was open for 17% -> 0% of each run, Pallas kernels for 0% -> 0%
where the time goes in v1:
time: 132 us
  Pallas kernels  130 us (98%)
  local copies, waits for them, and re-layouts  1.67 us (1%)
    pallas_call x1, Pallas kernels, shards(): pl.pallas_call(functools.partial(kernel, sections, chips, width, tokens),...  130 us

profile of v1, /device:TPU:1, one launch (start us, length us, event | category | flops | bytes accessed | tf_op | source)
XLA Modules:
  0.0 131.7 jit_solution(1477213639838324771)
XLA Ops:
  0.0 130.0 %shard_map.118 = bf16[1,128,1024]{2,1,0:T(8,128)(2,1)} custom-call(bf16[1,128,1024]{2,1,0:T(8,128)(2,1)} %act.1, f32[1,1024]{1,0:T(1,128)} %gain.1, bf16[1,32,3072]{2,1,0:T(8,128)(2,1)} %in_w.1, f32[3,1,3072]{2,1,0:T(1,128)} %bitcast.3, f32[1,32,4096]{2,1,0:T(8,128)} %filt.1, bf16[1,32,1024]{2,1,0:T(8,128)(2,1)} %bitcast.2, ...), custom_call_target="tpu_custom_call" | custom-call | tf_op jit(solution)/shard_map/pallas_call | solution.py:416
  130.0 1.7 %copy.14 = bf16[1,128,1024]{2,1,0:T(8,128)(2,1)} copy(bf16[1,128,1024]{2,1,0:T(8,128)(2,1)} %shard_map.118) | data formatting | bytes 524288

commit v2 on v1

--- a/solution.py
+++ b/solution.py
@@ -49,7 +49,7 @@
     out,
     w, rows_in, halo_in, normed, feat, prod, chan, query, outer, spec, back_hi, back_lo, conv, ret,
     fil, g_all, gi_all, d_all, di_all, tw_cos, tw_sin, g_hi, g_lo, gi_hi, gi_lo, d_hi, d_lo, di_hi, di_lo,
-    ring_send, ring_recv, own_sem, relay_send, relay_recv, to_send, to_recv, back_send, back_recv,
+    ring_send, ring_recv, pair_send, pair_recv, own_sem, relay_send, relay_recv, to_send, to_recv, back_send, back_recv,
     load_sem,
 ):
     parts = 2 * chips
@@ -81,16 +81,11 @@
         load.start()
 
     barrier = pltpu.get_barrier_semaphore()
-
-    def greet(offset, carry):
-        peer = lax.rem(me + offset, parts)
+    for peer in (left, right, sibling):
         pl.semaphore_signal(barrier, inc=1, device_id=(sec, peer), device_id_type=MESH)
-        return carry
-
-    lax.fori_loop(1, parts, greet, 0)
     pl.semaphore_signal(barrier, inc=1, device_id=(prev_sec, me), device_id_type=MESH)
     pl.semaphore_signal(barrier, inc=1, device_id=(prev_sec, prev_ctx), device_id_type=MESH)
-    pl.semaphore_wait(barrier, parts + 1)
+    pl.semaphore_wait(barrier, 5)
 
     relay = pltpu.make_async_remote_copy(
         act.at[0], rows_in, relay_send.at[0], relay_recv.at[0],
@@ -108,53 +103,68 @@
         in_w.at[0, :, pl.ds(0, width)], out_w.at[0],
     ]
 
-    def slot(kind, owner):
-        return w.at[kind, pl.ds(pl.multiple_of(owner * depth, depth), depth)]
-
-    def ring_copy(kind, source, owner, target):
+    half = width // 2
+    streams = [(0, 0, half), (1, 0, half), (0, half, half), (1, half, half), (2, 0, width), (3, 0, width)]
+    key_value, late = (0, 1, 2, 3), (4, 5)
+
+    def rows_of(owner):
+        return pl.ds(pl.multiple_of(owner * depth, depth), depth)
+
+    def ring_copy(stream, source, owner, target):
+        kind, first, count = streams[stream]
         return pltpu.make_async_remote_copy(
-            source, slot(kind, owner), ring_send.at[kind], ring_recv.at[kind, owner],
+            source, w.at[kind, rows_of(owner), pl.ds(first, count)],
+            ring_send.at[stream], ring_recv.at[stream, owner],
             device_id=(sec, target), device_id_type=MESH,
         )
 
-    def arrived(kind, owner):
-        pltpu.make_async_copy(slot(kind, owner), slot(kind, owner), ring_recv.at[kind, owner]).wait()
-
-    def ring_start(kind):
-        if hops_right:
-            ring_copy(kind, sources[kind], me, right).start()
-        if hops_left:
-            ring_copy(kind, sources[kind], me, left).start()
-        ring_copy(kind, sources[kind], me, sibling).start()
-        pltpu.make_async_copy(sources[kind], slot(kind, me), own_sem.at[kind]).start()
-
-    def ring_step(kind, step):
-        if step <= hops_right:
-            owner = at(chip - step, core)
-            arrived(kind, owner)
-            if step < hops_right:
-                ring_copy(kind, slot(kind, owner), owner, right).start()
-            ring_copy(kind, slot(kind, owner), owner, sibling).start()
-        if step <= hops_left:
-            owner = at(chip + step, core)
-            arrived(kind, owner)
-            if step < hops_left:
-                ring_copy(kind, slot(kind, owner), owner, left).start()
-            ring_copy(kind, slot(kind, owner), owner, sibling).start()
+    def sibling_copy(kind, source, owner):
+        return pltpu.make_async_remote_copy(
+            source, w.at[kind, rows_of(owner)], pair_send.at[kind], pair_recv.at[kind, lax.div(owner, 2)],
+            device_id=(sec, sibling), device_id_type=MESH,
+        )
+
+    def ring_start(group):
+        for stream in group:
+            kind, first, count = streams[stream]
+            own = sources[kind].at[:, pl.ds(first, count)]
+            if hops_right:
+                ring_copy(stream, own, me, right).start()
+            if hops_left:
+                ring_copy(stream, own, me, left).start()
+        for kind in sorted({streams[stream][0] for stream in group}):
+            sibling_copy(kind, sources[kind], me).start()
+            pltpu.make_async_copy(sources[kind], w.at[kind, rows_of(me)], own_sem.at[kind]).start()
+
+    def ring_step(group, step):
+        for stream in group:
+            kind, first, count = streams[stream]
+            for hops, owner, target in (
+                (hops_right, at(chip - step, core), right), (hops_left, at(chip + step, core), left)
+            ):
+                if step > hops:
+                    continue
+                here = w.at[kind, rows_of(owner), pl.ds(first, count)]
+                pltpu.make_async_copy(here, here, ring_recv.at[stream, owner]).wait()
+                if step < hops:
+                    ring_copy(stream, here, owner, target).start()
+                if first + count == width:
+                    sibling_copy(kind, w.at[kind, rows_of(owner)], owner).start()
 
     def ring_finish(kind):
-        pltpu.make_async_copy(sources[kind], slot(kind, me), own_sem.at[kind]).wait()
+        pltpu.make_async_copy(sources[kind], w.at[kind, rows_of(me)], own_sem.at[kind]).wait()
 
         def other(index, carry):
-            arrived(kind, 2 * index + 1 - core)
+            here = w.at[kind, rows_of(2 * index + 1 - core)]
+            pltpu.make_async_copy(here, here, pair_recv.at[kind, index]).wait()
             return carry
 
         lax.fori_loop(0, chips, other, 0)
 
-    ring_start(0)
+    ring_start(key_value)
     relay.start()
     relay_halo.start()
-    ring_start(1)
+    ring_start(late)
 
     def outer_rows(index, columns_high, columns_low):
         rows = pl.ds(pl.multiple_of(index * tile_o, tile_o), tile_o)
@@ -223,14 +233,16 @@
         norm_rows,
         lambda: (wait_loads(5, 2), split_table(di_all, di_hi, di_lo), split_table(gi_all, gi_hi, gi_lo)),
     ]
+    late_done = 0
     for step in range(1, steps + 1):
-        ring_step(0, step)
-        ring_step(1, step)
+        ring_step(key_value, step)
         if between:
             between.pop(0)()
+        if step % 2 == 0:
+            late_done += 1
+            ring_step(late, late_done)
     for piece in between:
         piece()
-    ring_start(2)
     ring_finish(0)
     ring_finish(1)
 
@@ -270,17 +282,14 @@
     lax.fori_loop(0, tiles, product_tile, 0)
     chan[me] = prod[me]
 
-    for step in range(1, steps + 1):
-        ring_step(2, step)
-    ring_start(3)
-    ring_finish(2)
+    while late_done < steps - 1:
+        late_done += 1
+        ring_step(late, late_done)
 
     def query_tile(index, carry):
         column = index * tile
         query[pl.ds(pl.multiple_of(column, tile), tile), :] = mixed(2, column, 0).T
         return carry
-
-    lax.fori_loop(0, tiles, query_tile, 0)
 
     def to_here(offset, carry):
         peer = lax.rem(me + offset, parts)
@@ -344,8 +353,11 @@
     lax.fori_loop(0, back_tiles, conv_tile, 0)
     ret[me] = conv[me]
 
-    for step in range(1, steps + 1):
-        ring_step(3, step)
+    while late_done < steps:
+        late_done += 1
+        ring_step(late, late_done)
+    ring_finish(2)
+    lax.fori_loop(0, tiles, query_tile, 0)
     ring_finish(3)
 
     def back_here(offset, carry):
@@ -363,10 +375,13 @@
 
     relay.wait_send()
     relay_halo.wait_send()
-    sent = (hops_right + hops_left + chips) * depth
+    for stream in key_value + late:
+        kind, first, count = streams[stream]
+        all_sent = w.at[kind, pl.ds(0, (hops_right + hops_left) * depth), pl.ds(first, count)]
+        pltpu.make_async_copy(all_sent, all_sent, ring_send.at[stream]).wait()
     for kind in range(4):
-        all_sent = w.at[kind, pl.ds(0, sent)]
-        pltpu.make_async_copy(all_sent, all_sent, ring_send.at[kind]).wait()
+        all_sent = w.at[kind, pl.ds(0, chips * depth)]
+        pltpu.make_async_copy(all_sent, all_sent, pair_send.at[kind]).wait()
     others = prod.at[pl.ds(0, parts - 1)]
     pltpu.make_async_copy(others, others, to_send).wait()
     others = conv.at[pl.ds(0, parts - 1)]
@@ -402,8 +417,10 @@
         pltpu.VMEM(long_filter.shape[1:], F32),
         *[pltpu.VMEM(table.shape, F32) for table in tables],
         *[pltpu.VMEM(table.shape, BF16) for table in tables[:4] for _ in range(2)],
+        pltpu.SemaphoreType.DMA((6,)),
+        pltpu.SemaphoreType.DMA((6, parts)),
         pltpu.SemaphoreType.DMA((4,)),
-        pltpu.SemaphoreType.DMA((4, parts)),
+        pltpu.SemaphoreType.DMA((4, chips)),
         pltpu.SemaphoreType.DMA((4,)),
         pltpu.SemaphoreType.DMA((2,)),
         pltpu.SemaphoreType.DMA((2,)),

time: 132 us -> 93.8 us (0.71)
  Pallas kernels: 130 us -> 91.7 us
    pallas_call x1, Pallas kernels: 130 us -> 91.7 us  [shards(): pl.pallas_call(functools.partial(kernel, sections, chips, width, tokens),...]
where the time goes in v2:
time: 93.8 us; the launch traced here: 93.4 us
  Pallas kernels  91.7 us (98%)
  local copies, waits for them, and re-layouts  1.67 us (2%)
    pallas_call x1, Pallas kernels, shards(): pl.pallas_call(functools.partial(kernel, sections, chips, width, tokens),...  91.7 us

profile of v2, /device:TPU:1, one launch (start us, length us, event | category | flops | bytes accessed | tf_op | source)
XLA Modules:
  0.0 93.4 jit_solution(12750557100255227581)
XLA Ops:
  0.0 91.7 %shard_map.118 = bf16[1,128,1024]{2,1,0:T(8,128)(2,1)} custom-call(bf16[1,128,1024]{2,1,0:T(8,128)(2,1)} %act.1, f32[1,1024]{1,0:T(1,128)} %gain.1, bf16[1,32,3072]{2,1,0:T(8,128)(2,1)} %in_w.1, f32[3,1,3072]{2,1,0:T(1,128)} %bitcast.3, f32[1,32,4096]{2,1,0:T(8,128)} %filt.1, bf16[1,32,1024]{2,1,0:T(8,128)(2,1)} %bitcast.2, ...), custom_call_target="tpu_custom_call" | custom-call | tf_op jit(solution)/shard_map/pallas_call | solution.py:433
  91.7 1.7 %copy.14 = bf16[1,128,1024]{2,1,0:T(8,128)(2,1)} copy(bf16[1,128,1024]{2,1,0:T(8,128)(2,1)} %shard_map.118) | data formatting | bytes 524288

commit v3 on v2

v3 whole, which is shorter than its diff:
```python
import functools
import math

import jax
import jax.numpy as jnp
import numpy as np
from jax import lax
from jax.experimental import pallas as pl
from jax.experimental.pallas import tpu as pltpu
from jax.sharding import PartitionSpec as P

MESH = pl.DeviceIdType.MESH
F32, BF16 = jnp.float32, jnp.bfloat16
HALO = 16
FEW = 8
PAIR = 2 * FEW


def transform_tables(parts, block):
    points = parts * block
    k = np.arange(parts)[:, None] + 0.25
    outer = 2.0 * math.pi * k * np.arange(parts)[None, :] / parts
    eye = np.eye(FEW)
    forward = np.concatenate([np.kron(np.cos(outer), eye), np.kron(-np.sin(outer), eye)], axis=0)
    inner = 2.0 * math.pi * np.outer(np.arange(block), np.arange(block)) / block
    cos, sin = np.cos(inner), np.sin(inner)
    inner_forward = np.block([[cos, -sin], [sin, cos]])
    inner_inverse = np.block([[cos, sin], [-sin, cos]])
    twist = np.repeat(2.0 * math.pi * k * np.arange(block)[None, :] / points, FEW, axis=0)
    tables = (forward, forward.T, inner_forward, inner_inverse, np.cos(twist), np.sin(twist))
    return [np.asarray(table, np.float32) for table in tables]


def split(value):
    high = value.astype(BF16)
    return high, (value - high.astype(F32)).astype(BF16)


def dot(a, b):
    return jnp.dot(a, b, preferred_element_type=F32)


def dot3(a_high, a_low, b_high, b_low):
    return dot(a_high, b_high) + (dot(a_high, b_low) + dot(a_low, b_high))


def kernel(
    sections, chips, width, tokens,
    act, gain, in_w, taps, filt, out_w, g_in, gi_in, d_in, di_in, tw_cos_in, tw_sin_in,
    out,
    w, rows_in, halo_in, normed, feat, prod, chan, query, outer, spec, back_hi, back_lo, conv, ret, gated,
    fil, g_all, gi_all, d_all, di_all, tw_cos, tw_sin, g_hi, g_lo, gi_hi, gi_lo, d_hi, d_lo, di_hi, di_lo,
    ring_send, ring_recv, pair_send, pair_recv, own_sem, relay_send, relay_recv, to_send, to_recv, back_send, back_recv,
    load_sem,
):
    parts = 2 * chips
    depth = width // parts
    block = tokens
    rows_k = parts * FEW
    pairs = depth // PAIR
    tile = min(256, width)
    sec, me = lax.axis_index("section"), lax.axis_index("ctx")
    core = lax.rem(me, 2)
    chip = lax.div(me, 2)

    def at(chip_index, core_index):
        return lax.rem(chip_index + 2 * chips, chips) * 2 + core_index

    right, left, sibling = at(chip + 1, core), at(chip - 1, core), at(chip, 1 - core)
    next_sec, prev_sec = lax.rem(sec + 1, sections), lax.rem(sec + sections - 1, sections)
    next_ctx, prev_ctx = lax.rem(me + 1, parts), lax.rem(me + parts - 1, parts)

    loads = [
        pltpu.make_async_copy(source, target, load_sem.at[slot])
        for slot, (source, target) in enumerate(
            [
                (filt.at[0], fil), (g_in, g_all), (d_in, d_all), (tw_cos_in, tw_cos), (tw_sin_in, tw_sin),
                (di_in, di_all), (gi_in, gi_all),
            ]
        )
    ]
    for load in loads:
        load.start()

    barrier = pltpu.get_barrier_semaphore()
    for peer in (left, right, sibling):
        pl.semaphore_signal(barrier, inc=1, device_id=(sec, peer), device_id_type=MESH)
    pl.semaphore_signal(barrier, inc=1, device_id=(prev_sec, me), device_id_type=MESH)
    pl.semaphore_signal(barrier, inc=1, device_id=(prev_sec, prev_ctx), device_id_type=MESH)
    pl.semaphore_wait(barrier, 5)

    relay = pltpu.make_async_remote_copy(
        act.at[0], rows_in, relay_send.at[0], relay_recv.at[0],
        device_id=(next_sec, me), device_id_type=MESH,
    )
    relay_halo = pltpu.make_async_remote_copy(
        act.at[0, pl.ds(tokens - HALO, HALO)], halo_in, relay_send.at[1], relay_recv.at[1],
        device_id=(next_sec, next_ctx), device_id_type=MESH,
    )

    hops = [(chips // 2, chips - 1 - chips // 2), (chips - 1 - chips // 2, chips // 2)]
    sources = [
        in_w.at[0, :, pl.ds(width, width)], in_w.at[0, :, pl.ds(2 * width, width)],
        in_w.at[0, :, pl.ds(0, width)], out_w.at[0],
    ]

    streams = [(0, 0, width), (1, 0, width), (2, 0, width), (3, 0, width)]
    key_value, late = (0, 1), (2, 3)

    def rows_of(owner):
        return pl.ds(pl.multiple_of(owner * depth, depth), depth)

    def ring_copy(stream, source, owner, target):
        kind, first, count = streams[stream]
        return pltpu.make_async_remote_copy(
            source, w.at[kind, rows_of(owner), pl.ds(first, count)],
            ring_send.at[stream], ring_recv.at[stream, owner],
            device_id=(sec, target), device_id_type=MESH,
        )

    def sibling_copy(kind, source, owner):
        return pltpu.make_async_remote_copy(
            source, w.at[kind, rows_of(owner)], pair_send.at[kind], pair_recv.at[kind, lax.div(owner, 2)],
            device_id=(sec, sibling), device_id_type=MESH,
        )

    def ring_start(group):
        for stream in group:
            kind, first, count = streams[stream]
            own = sources[kind].at[:, pl.ds(first, count)]
            for count, target in zip(hops[stream % 2], (right, left)):
                if count:
                    ring_copy(stream, own, me, target).start()
        for kind in sorted({streams[stream][0] for stream in group}):
            sibling_copy(kind, sources[kind], me).start()
            pltpu.make_async_copy(sources[kind], w.at[kind, rows_of(me)], own_sem.at[kind]).start()

    def ring_step(group, step):
        for stream in group:
            kind, first, count = streams[stream]
            ways = ((at(chip - step, core), right), (at(chip + step, core), left))
            for far, (owner, target) in zip(hops[stream % 2], ways):
                if step > far:
                    continue
                here = w.at[kind, rows_of(owner), pl.ds(first, count)]
                pltpu.make_async_copy(here, here, ring_recv.at[stream, owner]).wait()
                if step < far:
                    ring_copy(stream, here, owner, target).start()
                if first + count == width:
                    sibling_copy(kind, w.at[kind, rows_of(owner)], owner).start()

    def ring_finish(kind):
        pltpu.make_async_copy(sources[kind], w.at[kind, rows_of(me)], own_sem.at[kind]).wait()

        def other(index, carry):
            here = w.at[kind, rows_of(2 * index + 1 - core)]
            pltpu.make_async_copy(here, here, pair_recv.at[kind, index]).wait()
            return carry

        lax.fori_loop(0, chips, other, 0)

    ring_start(key_value)
    relay.start()
    relay_halo.start()
    ring_start(late)

    def outer_rows(pair, columns_high, columns_low):
        lanes = pl.ds(2 * block * pair, 2 * block)
        for index in range(2):
            rows = pl.ds(index * rows_k, rows_k)
            value = dot(g_hi[rows, :], columns_high) + dot(g_lo[rows, :], columns_high)
            if columns_low is not None:
                value = value + dot(g_hi[rows, :], columns_low)
            outer[rows, lanes] = value

    def inner_rows(group):
        lanes = pl.ds(group * block, block)
        real, imag = outer[pl.ds(0, rows_k), lanes], outer[pl.ds(rows_k, rows_k), lanes]
        cos, sin = tw_cos[...], tw_sin[...]
        turned = jnp.concatenate([real * cos + imag * sin, imag * cos - real * sin], axis=1)
        high, low = split(turned)
        return dot3(high, low, d_hi[...], d_lo[...])

    def filter_outer(pair):
        columns = [
            jnp.concatenate(
                [fil[pl.ds(group * FEW, FEW), pl.ds(n * block, block)] for n in range(parts)], axis=0
            )
            for group in (2 * pair, 2 * pair + 1)
        ]
        high, low = split(jnp.concatenate(columns, axis=1))
        outer_rows(pair, high, low)

    def filter_inner(group):
        spec[group] = inner_rows(group) * (1.0 / (parts * block))

    def norm(values, gain_row):
        values = values.astype(F32)
        scale = lax.rsqrt(jnp.mean(values * values, axis=-1, keepdims=True) + 1e-06)
        return values * scale * gain_row

    def norm_rows():
        relay.wait_recv()
        relay_halo.wait_recv()
        before = norm(halo_in[...], gain[...])
        normed[pl.ds(0, HALO), :] = jnp.where(me > 0, before, jnp.zeros_like(before)).astype(BF16)
        normed[pl.ds(HALO, tokens), :] = norm(rows_in[...], gain[...]).astype(BF16)

    def wait_loads(first, count):
        for load in loads[first : first + count]:
            load.wait()

    steps = chips // 2
    def split_table(whole, high, low):
        high[...], low[...] = split(whole[...])

    between = [
        lambda: (wait_loads(0, 2), split_table(g_all, g_hi, g_lo)),
        lambda: [filter_outer(pair) for pair in range(pairs)],
        lambda: (wait_loads(2, 3), split_table(d_all, d_hi, d_lo), filter_inner(0), filter_inner(1)),
        lambda: [filter_inner(group) for group in range(2, 2 * pairs)],
        norm_rows,
        lambda: (wait_loads(5, 2), split_table(di_all, di_hi, di_lo), split_table(gi_all, gi_hi, gi_lo)),
    ]
    late_done = 0
    for step in range(1, steps + 1):
        ring_step(key_value, step)
        if between:
            between.pop(0)()
        if step >= 2:
            late_done += 1
            ring_step(late, late_done)
    for piece in between:
        piece()
    ring_finish(0)
    ring_finish(1)

    def mixed(kind, column, place):
        columns = pl.ds(pl.multiple_of(column, tile), tile)
        feat[place] = dot(normed[...], w[kind, :, columns])
        base = (0 if kind == 2 else width * (kind + 1)) + column
        weights = [taps[i, :, pl.ds(pl.multiple_of(base, tile), tile)] for i in range(3)]
        value = weights[0] * feat[place, pl.ds(HALO, tokens), :]
        value = value + weights[1] * feat[place, pl.ds(HALO - 1, tokens), :]
        return value + weights[2] * feat[place, pl.ds(HALO - 2, tokens), :]

    tiles = width // tile
    per_tile = tile // depth

    def product_tile(index, carry):
        at_tile = lax.rem(lax.div(me, per_tile) + 1 + index, tiles)
        column = at_tile * tile
        value = (mixed(0, column, 0) * mixed(1, column, 1)).T.astype(BF16)
        first = pl.multiple_of(at_tile * per_tile, per_tile)
        prod[pl.ds(first, per_tile)] = value.reshape(per_tile, depth, tokens)

        lax.fori_loop(0, per_tile, lambda offset, inner: send(0, first + offset, inner), 0)
        return carry

    def over(source, target, send_sem, recv_sem):
        def send(pair, peer, carry):
            channels = pl.ds(pair * PAIR, PAIR)

            @pl.when(peer != me)
            def _():
                pltpu.make_async_remote_copy(
                    source.at[peer, channels], target.at[me, channels], send_sem.at[pair], recv_sem.at[pair, me],
                    device_id=(sec, peer), device_id_type=MESH,
                ).start()

            return carry

        def here(pair):
            def one(offset, carry):
                peer = lax.rem(me + offset, parts)
                landed = target.at[peer, pl.ds(pair * PAIR, PAIR)]
                pltpu.make_async_copy(landed, landed, recv_sem.at[pair, peer]).wait()
                return carry

            lax.fori_loop(1, parts, one, 0)

        def left_here():
            for pair in range(pairs):
                others = source.at[pl.ds(0, parts - 1), pl.ds(0, PAIR)]
                pltpu.make_async_copy(others, others, send_sem.at[pair]).wait()

        return send, here, left_here

    send, product_here, product_left = over(prod, chan, to_send, to_recv)
    send_back, conv_here, conv_left = over(conv, ret, back_send, back_recv)

    def to_all(send_one, pair):
        lax.fori_loop(1, parts, lambda offset, carry: send_one(pair, lax.rem(me + offset, parts), carry), 0)

    lax.fori_loop(0, tiles, product_tile, 0)
    for pair in range(1, pairs):
        to_all(send, pair)
    chan[me] = prod[me]

    def late_step():
        nonlocal late_done
        if late_done < steps:
            late_done += 1
            ring_step(late, late_done)

    late_step()

    def convolve(pair):
        data = chan[:, pl.ds(pair * PAIR, PAIR), :].astype(F32)
        columns = jnp.concatenate(
            [data[:, :FEW].reshape(rows_k, block), data[:, FEW:].reshape(rows_k, block)], axis=1
        )
        outer_rows(pair, columns.astype(BF16), None)
        for group in (2 * pair, 2 * pair + 1):
            lanes = pl.ds(group * block, block)
            data = inner_rows(group)
            real, imag = data[:, :block], data[:, block:]
            filter_real, filter_imag = spec[group, :, pl.ds(0, block)], spec[group, :, pl.ds(block, block)]
            points = jnp.concatenate(
                [real * filter_real - imag * filter_imag, real * filter_imag + imag * filter_real], axis=1
            )
            high, low = split(points)
            value = dot3(high, low, di_hi[...], di_lo[...])
            real, imag = value[:, :block], value[:, block:]
            cos, sin = tw_cos[...], tw_sin[...]
            above, below = pl.ds(0, rows_k), pl.ds(rows_k, rows_k)
            back_hi[above, lanes], back_lo[above, lanes] = split(real * cos - imag * sin)
            back_hi[below, lanes], back_lo[below, lanes] = split(imag * cos + real * sin)
        lanes = pl.ds(2 * block * pair, 2 * block)
        value = dot3(gi_hi[...], gi_lo[...], back_hi[:, lanes], back_lo[:, lanes])
        whole = jnp.concatenate(
            [value[:, :block].reshape(parts, FEW, block), value[:, block:].reshape(parts, FEW, block)], axis=1
        )
        conv[:, pl.ds(pair * PAIR, PAIR), :] = whole.astype(BF16)

    for pair in range(pairs):
        product_here(pair)
        convolve(pair)
        to_all(send_back, pair)
        late_step()
    ret[me] = conv[me]
    while late_done < steps:
        late_step()

    def query_tile(index, carry):
        value = mixed(2, index * tile, 0).T
        query[pl.ds(pl.multiple_of(index * per_tile, per_tile), per_tile)] = value.reshape(per_tile, depth, tokens)
        return carry

    ring_finish(2)
    lax.fori_loop(0, tiles, query_tile, 0)
    ring_finish(3)

    for pair in range(pairs):
        conv_here(pair)
        channels = pl.ds(pair * PAIR, PAIR)
        gated[:, channels, :] = (query[:, channels, :] * ret[:, channels, :].astype(F32)).astype(BF16)
    gates = gated[...].reshape(width, tokens)
    for index in range(tiles):
        span = pl.ds(index * tile, tile)
        mixing = dot(w[3, span, :], gates)
        out[0, :, span] = (rows_in[:, span].astype(F32) + mixing.T).astype(BF16)

    relay.wait_send()
    relay_halo.wait_send()
    for stream in key_value + late:
        kind, first, count = streams[stream]
        all_sent = w.at[kind, pl.ds(0, (chips - 1) * depth), pl.ds(first, count)]
        pltpu.make_async_copy(all_sent, all_sent, ring_send.at[stream]).wait()
    for kind in range(4):
        all_sent = w.at[kind, pl.ds(0, chips * depth)]
        pltpu.make_async_copy(all_sent, all_sent, pair_send.at[kind]).wait()
    product_left()
    conv_left()


def shards(activations, norm_gain, in_weight, short_weight, long_filter, out_weight):
    sections, parts = lax.axis_size("section"), lax.axis_size("ctx")
    chips = parts // 2
    tokens, width = activations.shape[1:]
    depth = width // parts
    rows_k = parts * FEW
    groups, pairs = depth // FEW, depth // PAIR
    tables = [jnp.asarray(table) for table in transform_tables(parts, tokens)]
    in_hbm = pl.BlockSpec(memory_space=pltpu.HBM)
    in_vmem = pl.BlockSpec(memory_space=pltpu.VMEM)
    tile = min(256, width)
    scratch = [
        pltpu.VMEM((4, width, width), BF16),
        pltpu.VMEM((tokens, width), BF16),
        pltpu.VMEM((HALO, width), BF16),
        pltpu.VMEM((HALO + tokens, width), BF16),
        pltpu.VMEM((2, HALO + tokens, tile), F32),
        pltpu.VMEM((parts, depth, tokens), BF16),
        pltpu.VMEM((parts, depth, tokens), BF16),
        pltpu.VMEM((parts, depth, tokens), F32),
        pltpu.VMEM((2 * rows_k, groups * tokens), F32),
        pltpu.VMEM((groups, rows_k, 2 * tokens), F32),
        pltpu.VMEM((2 * rows_k, groups * tokens), BF16),
        pltpu.VMEM((2 * rows_k, groups * tokens), BF16),
        pltpu.VMEM((parts, depth, tokens), BF16),
        pltpu.VMEM((parts, depth, tokens), BF16),
        pltpu.VMEM((parts, depth, tokens), BF16),
        pltpu.VMEM(long_filter.shape[1:], F32),
        *[pltpu.VMEM(table.shape, F32) for table in tables],
        *[pltpu.VMEM(table.shape, BF16) for table in tables[:4] for _ in range(2)],
        pltpu.SemaphoreType.DMA((4,)),
        pltpu.SemaphoreType.DMA((4, parts)),
        pltpu.SemaphoreType.DMA((4,)),
        pltpu.SemaphoreType.DMA((4, chips)),
        pltpu.SemaphoreType.DMA((4,)),
        pltpu.SemaphoreType.DMA((2,)),
        pltpu.SemaphoreType.DMA((2,)),
        pltpu.SemaphoreType.DMA((pairs,)),
        pltpu.SemaphoreType.DMA((pairs, parts)),
        pltpu.SemaphoreType.DMA((pairs,)),
        pltpu.SemaphoreType.DMA((pairs, parts)),
        pltpu.SemaphoreType.DMA((len(tables) + 1,)),
    ]
    return pl.pallas_call(
        functools.partial(kernel, sections, chips, width, tokens),
        out_shape=pltpu.VMEM(activations.shape, BF16),
        in_specs=[in_hbm, in_vmem, in_hbm, in_vmem] + [in_hbm] * (2 + len(tables)),
        out_specs=in_vmem,
        scratch_shapes=scratch,
        compiler_params=pltpu.CompilerParams(
            collective_id=0, has_side_effects=True, vmem_limit_bytes=63 * 1024 * 1024
        ),
    )(
        activations, norm_gain, in_weight, jnp.transpose(short_weight, (1, 0, 2)), long_filter,
        jnp.swapaxes(out_weight, 1, 2), *tables,
    )


def solution(mesh):
    return jax.shard_map(
        shards,
        mesh=mesh,
        in_specs=(
            P("section", "ctx", None),
            P("section", None),
            P("section", "ctx", None),
            P("section", None, None),
            P("section", "ctx", None),
            P("section", None, "ctx"),
        ),
        out_specs=P("section", "ctx", None),
        check_vma=False,
    )
```

time: 93.8 us -> 92.5 us (0.986)
  local copies, waits for them, and re-layouts: 1.67 us -> 0.71 us
    unnamed x1, local copies, waits for them, and re-layouts: 1.67 us -> 0.71 us
where the time goes in v3:
time: 92.5 us; the launch traced here: 92.3 us
  Pallas kernels  91.6 us (99%)
    pallas_call x1, Pallas kernels, shards(): pl.pallas_call(functools.partial(kernel, sections, chips, width, tokens),...  91.6 us

profile of v3, /device:TPU:1, one launch (start us, length us, event | category | flops | bytes accessed | tf_op | source)
XLA Modules:
  0.0 92.3 jit_solution(8673824064307774441)
XLA Ops:
  0.0 91.6 %shard_map.118 = bf16[1,128,1024]{2,1,0:T(8,128)(2,1)S(1)} custom-call(bf16[1,128,1024]{2,1,0:T(8,128)(2,1)} %act.1, f32[1,1024]{1,0:T(1,128)} %gain.1, bf16[1,32,3072]{2,1,0:T(8,128)(2,1)} %in_w.1, f32[3,1,3072]{2,1,0:T(1,128)} %bitcast.3, f32[1,32,4096]{2,1,0:T(8,128)} %filt.1, bf16[1,32,1024]{2,1,0:T(8,128)(2,1)} %bitcast.2, ...), custom_call_target="tpu_custom_call" | custom-call | tf_op jit(solution)/shard_map/pallas_call | solution.py:420
  91.6 0.7 copy.14

commit v4 on v3

--- a/solution.py
+++ b/solution.py
@@ -48,7 +48,7 @@
     sections, chips, width, tokens,
     act, gain, in_w, taps, filt, out_w, g_in, gi_in, d_in, di_in, tw_cos_in, tw_sin_in,
     out,
-    w, rows_in, halo_in, normed, feat, prod, chan, query, outer, spec, back_hi, back_lo, conv, ret, gated,
+    w, rows_in, halo_in, normed, feat, prod, chan, query, outer, spec, back_hi, back_lo, conv, ret,
     fil, g_all, gi_all, d_all, di_all, tw_cos, tw_sin, g_hi, g_lo, gi_hi, gi_lo, d_hi, d_lo, di_hi, di_lo,
     ring_send, ring_recv, pair_send, pair_recv, own_sem, relay_send, relay_recv, to_send, to_recv, back_send, back_recv,
     load_sem,
@@ -227,14 +227,11 @@
         ring_step(key_value, step)
         if between:
             between.pop(0)()
-        if step >= 2:
+        if 2 <= step < steps:
             late_done += 1
             ring_step(late, late_done)
     for piece in between:
         piece()
-    ring_finish(0)
-    ring_finish(1)
-
     def mixed(kind, column, place):
         columns = pl.ds(pl.multiple_of(column, tile), tile)
         feat[place] = dot(normed[...], w[kind, :, columns])
@@ -247,8 +244,13 @@
     tiles = width // tile
     per_tile = tile // depth
 
+    turns = [2, 1, 3, 0] if tiles == 4 else [*range(1, tiles), 0]
+
+    def quarter(turn):
+        return lax.rem(lax.div(me, per_tile) + turn, tiles)
+
     def product_tile(index, carry):
-        at_tile = lax.rem(lax.div(me, per_tile) + 1 + index, tiles)
+        at_tile = lax.rem(lax.div(me, per_tile) + 2 + index, tiles)
         column = at_tile * tile
         value = (mixed(0, column, 0) * mixed(1, column, 1)).T.astype(BF16)
         first = pl.multiple_of(at_tile * per_tile, per_tile)
@@ -271,13 +273,15 @@
             return carry
 
         def here(pair):
-            def one(offset, carry):
-                peer = lax.rem(me + offset, parts)
-                landed = target.at[peer, pl.ds(pair * PAIR, PAIR)]
-                pltpu.make_async_copy(landed, landed, recv_sem.at[pair, peer]).wait()
+            def one(peer, carry):
+                @pl.when(peer != me)
+                def _():
+                    landed = target.at[peer, pl.ds(pair * PAIR, PAIR)]
+                    pltpu.make_async_copy(landed, landed, recv_sem.at[pair, peer]).wait()
+
                 return carry
 
-            lax.fori_loop(1, parts, one, 0)
+            lax.fori_loop(0, parts, one, 0)
 
         def left_here():
             for pair in range(pairs):
@@ -290,11 +294,16 @@
     send_back, conv_here, conv_left = over(conv, ret, back_send, back_recv)
 
     def to_all(send_one, pair):
-        lax.fori_loop(1, parts, lambda offset, carry: send_one(pair, lax.rem(me + offset, parts), carry), 0)
-
+        for turn in turns:
+            first = quarter(turn) * per_tile
+            lax.fori_loop(
+                0, per_tile,
+                lambda offset, carry, first=first: send_one(pair, first + lax.rem(me + offset, per_tile), carry), 0,
+            )
+
+    ring_finish(0)
+    ring_finish(1)
     lax.fori_loop(0, tiles, product_tile, 0)
-    for pair in range(1, pairs):
-        to_all(send, pair)
     chan[me] = prod[me]
 
     def late_step():
@@ -304,6 +313,9 @@
             ring_step(late, late_done)
 
     late_step()
+    for pair in range(1, pairs):
+        to_all(send, pair)
+
 
     def convolve(pair):
         data = chan[:, pl.ds(pair * PAIR, PAIR), :].astype(F32)
@@ -353,9 +365,7 @@
 
     for pair in range(pairs):
         conv_here(pair)
-        channels = pl.ds(pair * PAIR, PAIR)
-        gated[:, channels, :] = (query[:, channels, :] * ret[:, channels, :].astype(F32)).astype(BF16)
-    gates = gated[...].reshape(width, tokens)
+    gates = (query[...] * ret[...].astype(F32)).astype(BF16).reshape(width, tokens)
     for index in range(tiles):
         span = pl.ds(index * tile, tile)
         mixing = dot(w[3, span, :], gates)
@@ -398,7 +408,6 @@
         pltpu.VMEM((groups, rows_k, 2 * tokens), F32),
         pltpu.VMEM((2 * rows_k, groups * tokens), BF16),
         pltpu.VMEM((2 * rows_k, groups * tokens), BF16),
-        pltpu.VMEM((parts, depth, tokens), BF16),
         pltpu.VMEM((parts, depth, tokens), BF16),
         pltpu.VMEM((parts, depth, tokens), BF16),
         pltpu.VMEM(long_filter.shape[1:], F32),

time: 92.5 us -> 88.9 us (0.961)
  Pallas kernels: 91.6 us -> 88 us
    pallas_call x1, Pallas kernels: 91.6 us -> 88 us  [shards(): pl.pallas_call(functools.partial(kernel, sections, chips, width, tokens),...]
where the time goes in v4:
time: 88.9 us; the launch traced here: 88.7 us
  Pallas kernels  88 us (99%)
    pallas_call x1, Pallas kernels, shards(): pl.pallas_call(functools.partial(kernel, sections, chips, width, tokens),...  88 us

profile of v4, /device:TPU:1, one launch (start us, length us, event | category | flops | bytes accessed | tf_op | source)
XLA Modules:
  0.0 88.7 jit_solution(2178788251506221050)
XLA Ops:
  0.0 88.0 %shard_map.118 = bf16[1,128,1024]{2,1,0:T(8,128)(2,1)S(1)} custom-call(bf16[1,128,1024]{2,1,0:T(8,128)(2,1)} %act.1, f32[1,1024]{1,0:T(1,128)} %gain.1, bf16[1,32,3072]{2,1,0:T(8,128)(2,1)} %in_w.1, f32[3,1,3072]{2,1,0:T(1,128)} %bitcast.3, f32[1,32,4096]{2,1,0:T(8,128)} %filt.1, bf16[1,32,1024]{2,1,0:T(8,128)(2,1)} %bitcast.2, ...), custom_call_target="tpu_custom_call" | custom-call | tf_op jit(solution)/shard_map/pallas_call | solution.py:429
  88.0 0.7 copy.14

commit v5 on v4

--- a/solution.py
+++ b/solution.py
@@ -46,10 +46,10 @@
 
 def kernel(
     sections, chips, width, tokens,
-    act, gain, in_w, taps, filt, out_w, g_in, gi_in, d_in, di_in, tw_cos_in, tw_sin_in,
+    act, gain_in, in_w, taps_in, filt, out_w, g_in, gi_in, d_in, di_in, tw_cos_in, tw_sin_in,
     out,
     w, rows_in, halo_in, normed, feat, prod, chan, query, outer, spec, back_hi, back_lo, conv, ret,
-    fil, g_all, gi_all, d_all, di_all, tw_cos, tw_sin, g_hi, g_lo, gi_hi, gi_lo, d_hi, d_lo, di_hi, di_lo,
+    gain, taps, fil, g_all, gi_all, d_all, di_all, tw_cos, tw_sin, g_hi, g_lo, gi_hi, gi_lo, d_hi, d_lo, di_hi, di_lo,
     ring_send, ring_recv, pair_send, pair_recv, own_sem, relay_send, relay_recv, to_send, to_recv, back_send, back_recv,
     load_sem,
 ):
@@ -69,18 +69,6 @@
     right, left, sibling = at(chip + 1, core), at(chip - 1, core), at(chip, 1 - core)
     next_sec, prev_sec = lax.rem(sec + 1, sections), lax.rem(sec + sections - 1, sections)
     next_ctx, prev_ctx = lax.rem(me + 1, parts), lax.rem(me + parts - 1, parts)
-
-    loads = [
-        pltpu.make_async_copy(source, target, load_sem.at[slot])
-        for slot, (source, target) in enumerate(
-            [
-                (filt.at[0], fil), (g_in, g_all), (d_in, d_all), (tw_cos_in, tw_cos), (tw_sin_in, tw_sin),
-                (di_in, di_all), (gi_in, gi_all),
-            ]
-        )
-    ]
-    for load in loads:
-        load.start()
 
     barrier = pltpu.get_barrier_semaphore()
     for peer in (left, right, sibling):
@@ -164,6 +152,18 @@
     relay_halo.start()
     ring_start(late)
 
+    loads = [
+        pltpu.make_async_copy(source, target, load_sem.at[slot])
+        for slot, (source, target) in enumerate(
+            [
+                (filt.at[0], fil), (g_in, g_all), (d_in, d_all), (tw_cos_in, tw_cos), (tw_sin_in, tw_sin),
+                (di_in, di_all), (gi_in, gi_all), (gain_in, gain), (taps_in, taps),
+            ]
+        )
+    ]
+    for load in loads:
+        load.start()
+
     def outer_rows(pair, columns_high, columns_low):
         lanes = pl.ds(2 * block * pair, 2 * block)
         for index in range(2):
@@ -200,6 +200,7 @@
         return values * scale * gain_row
 
     def norm_rows():
+        wait_loads(7, 2)
         relay.wait_recv()
         relay_halo.wait_recv()
         before = norm(halo_in[...], gain[...])
@@ -410,6 +411,8 @@
         pltpu.VMEM((2 * rows_k, groups * tokens), BF16),
         pltpu.VMEM((parts, depth, tokens), BF16),
         pltpu.VMEM((parts, depth, tokens), BF16),
+        pltpu.VMEM(norm_gain.shape, F32),
+        pltpu.VMEM((3, 1, 3 * width), F32),
         pltpu.VMEM(long_filter.shape[1:], F32),
         *[pltpu.VMEM(table.shape, F32) for table in tables],
         *[pltpu.VMEM(table.shape, BF16) for table in tables[:4] for _ in range(2)],
@@ -424,12 +427,12 @@
         pltpu.SemaphoreType.DMA((pairs, parts)),
         pltpu.SemaphoreType.DMA((pairs,)),
         pltpu.SemaphoreType.DMA((pairs, parts)),
-        pltpu.SemaphoreType.DMA((len(tables) + 1,)),
+        pltpu.SemaphoreType.DMA((len(tables) + 3,)),
     ]
     return pl.pallas_call(
         functools.partial(kernel, sections, chips, width, tokens),
         out_shape=pltpu.VMEM(activations.shape, BF16),
-        in_specs=[in_hbm, in_vmem, in_hbm, in_vmem] + [in_hbm] * (2 + len(tables)),
+        in_specs=[in_hbm] * (6 + len(tables)),
         out_specs=in_vmem,
         scratch_shapes=scratch,
         compiler_params=pltpu.CompilerParams(

time: 88.9 us -> 87.9 us (0.989)
  Pallas kernels: 88 us -> 87.1 us
where the time goes in v5:
time: 87.9 us; the launch traced here: 87.8 us
  Pallas kernels  87.1 us (99%)
    pallas_call x1, Pallas kernels, shards(): pl.pallas_call(functools.partial(kernel, sections, chips, width, tokens),...  87.1 us

profile of v5, /device:TPU:1, one launch (start us, length us, event | category | flops | bytes accessed | tf_op | source)
XLA Modules:
  0.0 87.8 jit_solution(14315954354504784005)
XLA Ops:
  0.0 87.1 %shard_map.118 = bf16[1,128,1024]{2,1,0:T(8,128)(2,1)S(1)} custom-call(bf16[1,128,1024]{2,1,0:T(8,128)(2,1)} %act.1, f32[1,1024]{1,0:T(1,128)} %gain_in.1, bf16[1,32,3072]{2,1,0:T(8,128)(2,1)} %in_w.1, f32[3,1,3072]{2,1,0:T(1,128)} %bitcast.3, f32[1,32,4096]{2,1,0:T(8,128)} %filt.1, bf16[1,32,1024]{2,1,0:T(8,128)(2,1)} %bitcast.2, ...), custom_call_target="tpu_custom_call" | custom-call | tf_op jit(solution)/shard_map/pallas_call | solution.py:432
  87.1 0.7 copy.14

commit v6 on v5

--- a/solution.py
+++ b/solution.py
@@ -108,7 +108,7 @@
 
     def sibling_copy(kind, source, owner):
         return pltpu.make_async_remote_copy(
-            source, w.at[kind, rows_of(owner)], pair_send.at[kind], pair_recv.at[kind, lax.div(owner, 2)],
+            source, w.at[kind, rows_of(owner)], pair_send.at[kind], pair_recv.at[kind],
             device_id=(sec, sibling), device_id_type=MESH,
         )
 
@@ -140,12 +140,8 @@
     def ring_finish(kind):
         pltpu.make_async_copy(sources[kind], w.at[kind, rows_of(me)], own_sem.at[kind]).wait()
 
-        def other(index, carry):
-            here = w.at[kind, rows_of(2 * index + 1 - core)]
-            pltpu.make_async_copy(here, here, pair_recv.at[kind, index]).wait()
-            return carry
-
-        lax.fori_loop(0, chips, other, 0)
+        landed = w.at[kind, pl.ds(0, chips * depth)]
+        pltpu.make_async_copy(landed, landed, pair_recv.at[kind]).wait()
 
     ring_start(key_value)
     relay.start()
@@ -267,22 +263,15 @@
             @pl.when(peer != me)
             def _():
                 pltpu.make_async_remote_copy(
-                    source.at[peer, channels], target.at[me, channels], send_sem.at[pair], recv_sem.at[pair, me],
+                    source.at[peer, channels], target.at[me, channels], send_sem.at[pair], recv_sem.at[pair],
                     device_id=(sec, peer), device_id_type=MESH,
                 ).start()
 
             return carry
 
         def here(pair):
-            def one(peer, carry):
-                @pl.when(peer != me)
-                def _():
-                    landed = target.at[peer, pl.ds(pair * PAIR, PAIR)]
-                    pltpu.make_async_copy(landed, landed, recv_sem.at[pair, peer]).wait()
-
-                return carry
-
-            lax.fori_loop(0, parts, one, 0)
+            landed = target.at[pl.ds(0, parts - 1), pl.ds(0, PAIR)]
+            pltpu.make_async_copy(landed, landed, recv_sem.at[pair]).wait()
 
         def left_here():
             for pair in range(pairs):
@@ -419,14 +408,14 @@
         pltpu.SemaphoreType.DMA((4,)),
         pltpu.SemaphoreType.DMA((4, parts)),
         pltpu.SemaphoreType.DMA((4,)),
-        pltpu.SemaphoreType.DMA((4, chips)),
+        pltpu.SemaphoreType.DMA((4,)),
         pltpu.SemaphoreType.DMA((4,)),
         pltpu.SemaphoreType.DMA((2,)),
         pltpu.SemaphoreType.DMA((2,)),
         pltpu.SemaphoreType.DMA((pairs,)),
-        pltpu.SemaphoreType.DMA((pairs, parts)),
         pltpu.SemaphoreType.DMA((pairs,)),
-        pltpu.SemaphoreType.DMA((pairs, parts)),
+        pltpu.SemaphoreType.DMA((pairs,)),
+        pltpu.SemaphoreType.DMA((pairs,)),
         pltpu.SemaphoreType.DMA((len(tables) + 3,)),
     ]
     return pl.pallas_call(

time: 87.9 us -> 86.6 us (0.985)
  Pallas kernels: 87.1 us -> 85.8 us
    pallas_call x1, Pallas kernels: 87.1 us -> 85.8 us  [shards(): pl.pallas_call(functools.partial(kernel, sections, chips, width, tokens),...]
where the time goes in v6:
time: 86.6 us; the launch traced here: 86.5 us
  Pallas kernels  85.8 us (99%)
    pallas_call x1, Pallas kernels, shards(): pl.pallas_call(functools.partial(kernel, sections, chips, width, tokens),...  85.8 us

profile of v6, /device:TPU:1, one launch (start us, length us, event | category | flops | bytes accessed | tf_op | source)
XLA Modules:
  0.0 86.5 jit_solution(396328972525932688)
XLA Ops:
  0.0 85.8 %shard_map.118 = bf16[1,128,1024]{2,1,0:T(8,128)(2,1)S(1)} custom-call(bf16[1,128,1024]{2,1,0:T(8,128)(2,1)} %act.1, f32[1,1024]{1,0:T(1,128)} %gain_in.1, bf16[1,32,3072]{2,1,0:T(8,128)(2,1)} %in_w.1, f32[3,1,3072]{2,1,0:T(1,128)} %bitcast.3, f32[1,32,4096]{2,1,0:T(8,128)} %filt.1, bf16[1,32,1024]{2,1,0:T(8,128)(2,1)} %bitcast.2, ...), custom_call_target="tpu_custom_call" | custom-call | tf_op jit(solution)/shard_map/pallas_call | solution.py:421
  85.8 0.7 copy.14

commit v7 on v6

--- a/solution.py
+++ b/solution.py
@@ -253,7 +253,7 @@
         first = pl.multiple_of(at_tile * per_tile, per_tile)
         prod[pl.ds(first, per_tile)] = value.reshape(per_tile, depth, tokens)
 
-        lax.fori_loop(0, per_tile, lambda offset, inner: send(0, first + offset, inner), 0)
+        lax.fori_loop(0, per_tile, lambda offset, inner: send(0, first + offset, inner), 0, unroll=True)
         return carry
 
     def over(source, target, send_sem, recv_sem):
@@ -289,6 +289,7 @@
             lax.fori_loop(
                 0, per_tile,
                 lambda offset, carry, first=first: send_one(pair, first + lax.rem(me + offset, per_tile), carry), 0,
+                unroll=True,
             )
 
     ring_finish(0)

time: 86.6 us -> 86.6 us (level)
  no operation moved by 1% of the time
where the time goes in v7:
time: 86.6 us; the launch traced here: 86.5 us
  Pallas kernels  85.8 us (99%)
    pallas_call x1, Pallas kernels, shards(): pl.pallas_call(functools.partial(kernel, sections, chips, width, tokens),...  85.8 us

profile of v7, /device:TPU:1, one launch (start us, length us, event | category | flops | bytes accessed | tf_op | source)
XLA Modules:
  0.0 86.5 jit_solution(17483144218513550558)
XLA Ops:
  0.0 85.8 %shard_map.118 = bf16[1,128,1024]{2,1,0:T(8,128)(2,1)S(1)} custom-call(bf16[1,128,1024]{2,1,0:T(8,128)(2,1)} %act.1, f32[1,1024]{1,0:T(1,128)} %gain_in.1, bf16[1,32,3072]{2,1,0:T(8,128)(2,1)} %in_w.1, f32[3,1,3072]{2,1,0:T(1,128)} %bitcast.3, f32[1,32,4096]{2,1,0:T(8,128)} %filt.1, bf16[1,32,1024]{2,1,0:T(8,128)(2,1)} %bitcast.2, ...), custom_call_target="tpu_custom_call" | custom-call | tf_op jit(solution)/shard_map/pallas_call | solution.py:422
  85.8 0.7 copy.14
